TPU v7x, 32 devices: a whole 2x2x4 slice. The times are simulated.
32 devices in a mesh: grp: 2 (over y), kb: 4 (over z), gb: 4 (over x, core).
Axes of the slice: x: 2, y: 2, z: 4, core: 2. Of those that a mesh axis runs over, the one named last changes fastest.
Arguments:
- amplitudes: float32 [4, 384, 16], P('grp', 'kb'), parts along dimension 0, may hold values from -6 to 6
- pulse_field: float32 [4], P('grp'), parts along dimension 0, may hold values from -2 to 2
- pair_density: bfloat16 [2, 384, 16, 2000], P(None, 'kb', None, 'gb'), may hold values from -6 to 6
- energies: float32 [384, 16], P('kb'), may hold values from 1 to 3
- dipoles: float32 [2, 384, 16], P(None, 'kb'), may hold values from -6 to 6
- coulomb: float32 [2000], P('gb'), may hold values from 0.5 to 2
- screened: float32 [16, 2000], P(None, 'gb'), may hold values from 0.5 to 2
- partners: int32 [384, 8], P('kb'), may hold values from 0 to 383, as said below
- shells: int32 [384, 8], P('kb'), may hold values from 0 to 15
- counts: int32 [384], P('kb'), may hold values from 1 to 8
Outputs:
- advanced: float32 [4, 384, 16], P('grp', 'kb'), parts along dimension 0
There are 2 independent parts, one for each index of `grp`. A program takes and returns all parts, laid end to end along the dimension named above; an argument that names none is the same for every part. Nothing has to cross between parts.
Inputs may be any that keep to these rules, and one draw needn't show every extreme that they name: The partners of a k point of block b (k // 96 = b) lie in blocks b, b - 1, b + 1 and b + 2, modulo 4; the partners of the k points of one block name exactly 24 distinct k points of each of these four blocks, and the first slot alone already names all of them; the partners of one k point are distinct.
All inputs are finite; a program needn't handle non-finite values.
Results may differ from a plain program's by a relative error of at most 0.0042.
Values may be sent and summed in bfloat16 or wider, within the bound.
A program may use at most 64 MiB of HBM per device.

v0:
```python
import math

import jax
import jax.numpy as jnp
from jax import lax
from jax.sharding import PartitionSpec as P

CAP = 24


time_step = 0.25


def body(
    amplitudes,
    pulse_field,
    pair_density,
    energies,
    dipoles,
    coulomb,
    screened,
    partners,
    shells,
    counts,
):
    k_rows, partner_slots = partners.shape
    pair_count = amplitudes.shape[2]
    g_local = coulomb.shape[0]
    shell_count = screened.shape[0]
    block_count = lax.axis_size("kb")
    g_blocks = lax.axis_size("gb")
    device_index = lax.axis_index("kb")
    offsets = jnp.array([0, block_count - 1, 1, block_count // 2], jnp.int32)
    sources = (device_index + offsets) % block_count
    source_block = partners // k_rows
    local_row = partners % k_rows
    distance = (source_block - device_index) % block_count
    source_slot = jnp.where(
        distance == 0, 0, jnp.where(distance == block_count - 1, 1, jnp.where(distance == 1, 2, 3))
    )
    flat_key = (source_slot * k_rows + local_row).reshape(-1)
    matches = (flat_key[:, None] == jnp.arange(4 * k_rows, dtype=jnp.int32)[None, :]).astype(
        jnp.int32
    )
    needed = (jnp.sum(matches, axis=0) > 0).astype(jnp.int32).reshape(4, k_rows)
    ranks = jnp.cumsum(needed, axis=1) - 1
    chosen = needed[:, :, None] * (
        ranks[:, :, None] == jnp.arange(CAP, dtype=jnp.int32)[None, None, :]
    ).astype(jnp.int32)
    request = jnp.sum(chosen * jnp.arange(k_rows, dtype=jnp.int32)[None, :, None], axis=1)
    position = source_slot.reshape(-1) * CAP + jnp.take(ranks.reshape(-1), flat_key)
    marks = (jnp.arange(block_count, dtype=jnp.int32)[:, None] == sources[None, :]).astype(
        jnp.int32
    )
    asked = jnp.sum(marks[:, :, None] * request[None, :, :], axis=1)
    given = lax.all_to_all(asked, "kb", split_axis=0, concat_axis=0, tiled=True)

    def fetch(sent_rows):
        outgoing = jnp.take(sent_rows, given.reshape(-1), axis=0).reshape(
            block_count, CAP, 2 * g_local
        )
        arrived = lax.all_to_all(outgoing, "kb", split_axis=0, concat_axis=0, tiled=True)
        return jnp.take(arrived, sources, axis=0)

    shell_onehot = (
        shells.reshape(-1)[:, None] == jnp.arange(shell_count, dtype=jnp.int32)[None, :]
    ).astype(jnp.float32)
    live_mask = (jnp.arange(partner_slots, dtype=jnp.int32)[None, :] < counts[:, None]).astype(
        jnp.float32
    )
    weights = jnp.dot(shell_onehot, screened, precision=lax.Precision.HIGHEST) * live_mask.reshape(
        -1, 1
    )
    exchange_weight = 2.0 / math.sqrt(pair_count * k_rows * block_count)
    direct_weight = 1.0 / math.sqrt(pair_count * partner_slots)
    g_scale = 1.0 / math.sqrt(g_local * g_blocks)

    def derivative(amps, efield):
        rounded_amp = amps.astype(jnp.bfloat16)
        dens_real = jnp.einsum(
            "kcg,kc->kg", pair_density[0], rounded_amp[0], preferred_element_type=jnp.float32
        ) - jnp.einsum(
            "kcg,kc->kg", pair_density[1], rounded_amp[1], preferred_element_type=jnp.float32
        )
        dens_imag = jnp.einsum(
            "kcg,kc->kg", pair_density[0], rounded_amp[1], preferred_element_type=jnp.float32
        ) + jnp.einsum(
            "kcg,kc->kg", pair_density[1], rounded_amp[0], preferred_element_type=jnp.float32
        )
        total_real, total_imag = lax.psum(
            (jnp.sum(dens_real, axis=0), jnp.sum(dens_imag, axis=0)), "kb"
        )
        sent_rows = jnp.concatenate([dens_real, dens_imag], axis=1).astype(jnp.bfloat16)
        received = fetch(sent_rows).reshape(4 * CAP, 2 * g_local)
        pulled = jnp.take(received, position, axis=0)
        summed_real = jnp.sum(
            (pulled[:, :g_local] * weights).reshape(k_rows, partner_slots, g_local), axis=1
        )
        summed_imag = jnp.sum(
            (pulled[:, g_local:] * weights).reshape(k_rows, partner_slots, g_local), axis=1
        )
        forcing_real = (
            exchange_weight * coulomb[None, :] * total_real[None, :] - direct_weight * summed_real
        ).astype(jnp.bfloat16)
        forcing_imag = (
            exchange_weight * coulomb[None, :] * total_imag[None, :] - direct_weight * summed_imag
        ).astype(jnp.bfloat16)
        proj_real = (
            jnp.einsum(
                "kcg,kg->kc", pair_density[0], forcing_real, preferred_element_type=jnp.float32
            )
            + jnp.einsum(
                "kcg,kg->kc", pair_density[1], forcing_imag, preferred_element_type=jnp.float32
            )
        ) * g_scale
        proj_imag = (
            jnp.einsum(
                "kcg,kg->kc", pair_density[0], forcing_imag, preferred_element_type=jnp.float32
            )
            - jnp.einsum(
                "kcg,kg->kc", pair_density[1], forcing_real, preferred_element_type=jnp.float32
            )
        ) * g_scale
        proj_real, proj_imag = lax.psum((proj_real, proj_imag), "gb")
        deriv_real = energies * amps[1] + proj_imag - efield * dipoles[1]
        deriv_imag = -(energies * amps[0] + proj_real - efield * dipoles[0])
        return jnp.stack([deriv_real, deriv_imag])

    half = amplitudes + 0.5 * time_step * derivative(amplitudes, pulse_field[0])
    return amplitudes + time_step * derivative(half, pulse_field[1])


def solution(mesh):
    in_specs = (
        P("grp", "kb", None),
        P("grp"),
        P(None, "kb", None, "gb"),
        P("kb", None),
        P(None, "kb", None),
        P("gb"),
        P(None, "gb"),
        P("kb", None),
        P("kb", None),
        P("kb"),
    )
    out_specs = P("grp", "kb", None)
    return jax.shard_map(body, mesh=mesh, in_specs=in_specs, out_specs=out_specs, check_vma=False)
```

profile of v0, /device:TPU:0, one launch (start us, length us, event | category | flops | bytes accessed | tf_op | source)
XLA Modules:
  0.0 146.1 jit_solution(7672443580075207414)
XLA Ops:
  0.0 0.7 broadcast_multiply_fusion
  0.9 0.2 convert_reduce_fusion
  1.2 0.3 reduce_window_sum.11
  1.6 0.7 compare_and_fusion.1
  2.3 0.7 multiply_reduce_fusion.1
  3.0 6.3 %all-to-all-start = ((s32[4,1,24]{2,1,0:T(1,128)}), s32[4,1,24]{2,1,0:T(1,128)S(1)}, u32[]{:S(2)}, u32[]{:S(2)}) async-start(s32[4,1,24]{2,1,0:T(1,128)} %bitcast.10), calls=%async_computation | async-start | bytes 4096 | tf_op jit(solution)/shard_map/all_to_all | solution.py:56
  9.3 0.7 convert_element_type.65
  10.2 2.6 %fusion.14 = f32[96,1,500]{2,1,0:T(1,128)} fusion(bf16[96,16,1]{1,2,0:T(2,128)(2,1)S(1)} %copy.48, bf16[2,96,16,500]{3,2,1,0:T(8,128)(2,1)} %param.19), kind=kOutput, calls=%fused_computation.25 | convolution fusion | flops 1536000 | bytes 1767936 | tf_op jit(solution)/shard_map/kcg,kc->kg/dot_general | solution.py:87
  12.7 2.4 %fusion.28 = f32[96,1,500]{2,1,0:T(1,128)} fusion(bf16[96,16,1]{1,2,0:T(2,128)(2,1)S(1)} %copy.48, bf16[2,96,16,500]{3,2,1,0:T(8,128)(2,1)} %param.19), kind=kOutput, calls=%fused_computation.39 | convolution fusion | flops 1536000 | bytes 1767936 | tf_op jit(solution)/shard_map/kcg,kc->kg/dot_general | solution.py:80
  15.3 1.0 fusion.12
  16.3 1.0 fusion.30
  17.9 0.6 fusion.99
  18.5 1.3 fusion.62
  19.9 5.0 %gather_fusion = s32[768]{0:T(1024)S(1)} fusion(s32[384]{0:T(512)S(1)} %sub.80, s32[1024]{0:T(1024)S(1)} %pad_clamp_fusion.3), kind=kCustom, calls=%fused_computation.6 | custom fusion | bytes 9216 | tf_op jit(solution)/shard_map/jit(_take)/gather | solution.py:51
  25.0 12.2 %all-reduce.3 = (f32[500]{0:T(512)S(1)}, f32[500]{0:T(512)S(1)}) all-reduce(f32[500]{0:T(512)S(1)} %get-tuple-element.32, f32[500]{0:T(512)S(1)} %get-tuple-element.52), channel_id=1, replica_groups=mesh['grp'=2,'kb'=4,'gb'=4] {'kb'}, use_global_device_ids=true, to_apply=%region_1.2 | all-reduce | flops 1000 | bytes 8000 | tf_op jit(solution)/shard_map/psum | solution.py:90
  37.5 0.5 broadcast.181
  38.0 0.7 reduce.5
  38.8 1.5 gather_fusion.1
  40.2 1.7 %broadcast_select_fusion.5 = bf16[96,1000]{1,0:T(8,128)(2,1)} fusion(bf16[96,1000]{1,0:T(8,128)(2,1)} %gather_fusion.1, pred[96]{0:T(512)(128)(4,1)S(1)} %compare_and_fusion.2), kind=kLoop, calls=%fused_computation.83 | loop fusion | flops 96000 | bytes 384096 | tf_op jit(solution)/shard_map/jit(_take)/select_n | solution.py:59
  41.9 3.4 %all-to-all-start.1 = ((bf16[4,24,1000]{2,1,0:T(8,128)(2,1)}), bf16[4,24,1000]{2,1,0:T(8,128)(2,1)S(1)}, u32[]{:S(2)}, u32[]{:S(2)}) async-start(bf16[4,24,1000]{2,1,0:T(8,128)(2,1)} %bitcast.211), calls=%async_computation.1 | async-start | bytes 393216 | tf_op jit(solution)/shard_map/all_to_all | solution.py:62
  45.3 6.2 %all-to-all-done.1 = bf16[4,24,1000]{2,1,0:T(8,128)(2,1)S(1)} async-done(((bf16[4,24,1000]{2,1,0:T(8,128)(2,1)}), bf16[4,24,1000]{2,1,0:T(8,128)(2,1)S(1)}, u32[]{:S(2)}, u32[]{:S(2)}) %all-to-all-start.1) | async-done | bytes 192032 | tf_op jit(solution)/shard_map/all_to_all | solution.py:62
  51.5 1.2 gather_fusion.2
  52.7 1.0 broadcast_select_fusion.3
  53.7 3.6 %gather_fusion.3 = bf16[768,1000]{1,0:T(8,128)(2,1)} fusion(bf16[96,1000]{1,0:T(8,128)(2,1)S(1)} %bitcast.209, s32[1024]{0:T(1024)S(1)} %pad_clamp_fusion), kind=kCustom, calls=%fused_computation.2.clone | custom fusion | bytes 3075072 | tf_op jit(solution)/shard_map/jit(_take)/gather | solution.py:95
  57.3 2.7 %copy.39 = bf16[768,1000]{0,1:T(8,128)(2,1)} copy(bf16[768,1000]{1,0:T(8,128)(2,1)} %gather_fusion.3) | data formatting | bytes 3072000 | tf_op jit(solution)/shard_map/jit(_take)/gather | solution.py:95
  60.0 1.5 %broadcast_select_fusion.1 = bf16[768,1000]{0,1:T(8,128)(2,1)S(1)} fusion(bf16[768,1000]{0,1:T(8,128)(2,1)} %copy.39, pred[768]{0:T(1024)(128)(4,1)S(1)} %get-tuple-element.18), kind=kLoop, calls=%fused_computation.48 | loop fusion | flops 768000 | bytes 3072768 | tf_op jit(solution)/shard_map/jit(_take)/select_n | solution.py:95
  61.5 3.5 %convert_multiply_fusion.2 = (f32[768,500]{0,1:T(8,128)}, f32[768,500]{0,1:T(8,128)}, f32[768,500]{0,1:T(8,128)}) fusion(bf16[768,1000]{0,1:T(8,128)(2,1)S(1)} %broadcast_select_fusion.1, f32[768]{0:T(1024)S(1)} %reshape.174, f32[16,500]{1,0:T(8,128)S(1)} %copy-done, s32[768]{0:T(1024)S(1)} %eq.90), kind=kOutput, calls=%fused_computation.45 | convolution fusion | flops 75660288 | bytes 6182144 | tf_op jit(solution)/shard_map/dot_general | solution.py:71
  65.0 3.0 %copy.42 = f32[768,500]{1,0:T(8,128)} copy(f32[768,500]{0,1:T(8,128)} %get-tuple-element.24) | data formatting | bytes 3072000 | tf_op jit(solution)/shard_map/mul | solution.py:97
  68.0 1.9 %bitcast_reduce_fusion.2 = f32[96,500]{1,0:T(8,128)S(1)} fusion(f32[768,500]{1,0:T(8,128)} %copy.42), kind=kLoop, calls=%fused_computation.9 | loop fusion | flops 336000 | bytes 1728000 | tf_op jit(solution)/shard_map/reduce_sum | solution.py:96
  69.9 0.6 fusion.10
  70.5 0.6 fusion.24
  71.1 3.0 %copy.41 = f32[768,500]{1,0:T(8,128)} copy(f32[768,500]{0,1:T(8,128)} %get-tuple-element.25) | data formatting | bytes 3072000 | tf_op jit(solution)/shard_map/mul | solution.py:100
  74.1 1.9 %bitcast_reduce_fusion.3 = f32[96,500]{1,0:T(8,128)S(1)} fusion(f32[768,500]{1,0:T(8,128)} %copy.41), kind=kLoop, calls=%fused_computation.10 | loop fusion | flops 336000 | bytes 1728000 | tf_op jit(solution)/shard_map/reduce_sum | solution.py:99
  76.0 0.6 fusion.26
  76.6 0.6 fusion.8
  77.5 10.1 %all-reduce.1 = (f32[96,16]{0,1:T(8,128)S(1)}, f32[96,16]{0,1:T(8,128)S(1)}) all-reduce(f32[96,16]{0,1:T(8,128)S(1)} %fusion.85, f32[96,16]{0,1:T(8,128)S(1)} %fusion.88), channel_id=1, replica_groups=mesh['grp'=2,'kb'=4,'gb'=4] {'gb'}, use_global_device_ids=true, to_apply=%region_11.15 | all-reduce | flops 3072 | bytes 24576 | tf_op jit(solution)/shard_map/psum | solution.py:124
  87.7 0.6 fusion.87
  88.5 1.0 fusion.4
  89.5 0.3 fusion.22
  90.0 0.3 fusion.20
  90.3 0.4 fusion.6
  90.7 0.2 copy-done.3
  91.1 1.5 gather_fusion.4
  92.5 1.7 %broadcast_select_fusion.4 = bf16[96,1000]{1,0:T(8,128)(2,1)} fusion(bf16[96,1000]{1,0:T(8,128)(2,1)} %gather_fusion.4, pred[96]{0:T(512)(128)(4,1)S(1)} %compare_and_fusion.2), kind=kLoop, calls=%fused_computation.82 | loop fusion | flops 96000 | bytes 384096 | tf_op jit(solution)/shard_map/jit(_take)/select_n | solution.py:59
  94.2 3.4 %all-to-all-start.2 = ((bf16[4,24,1000]{2,1,0:T(8,128)(2,1)}), bf16[4,24,1000]{2,1,0:T(8,128)(2,1)S(1)}, u32[]{:S(2)}, u32[]{:S(2)}) async-start(bf16[4,24,1000]{2,1,0:T(8,128)(2,1)} %bitcast.210), calls=%async_computation.2 | async-start | bytes 393216 | tf_op jit(solution)/shard_map/all_to_all | solution.py:62
  97.6 12.3 %all-reduce.2 = (f32[500]{0:T(512)S(1)}, f32[500]{0:T(512)S(1)}) all-reduce(f32[500]{0:T(512)S(1)} %get-tuple-element.28, f32[500]{0:T(512)S(1)} %get-tuple-element.26), channel_id=1, replica_groups=mesh['grp'=2,'kb'=4,'gb'=4] {'kb'}, use_global_device_ids=true, to_apply=%region_13.17 | all-reduce | flops 1000 | bytes 8000 | tf_op jit(solution)/shard_map/psum | solution.py:90
  109.9 1.2 gather_fusion.5
  111.1 1.0 broadcast_select_fusion.2
  112.1 3.6 %gather_fusion.6 = bf16[768,1000]{1,0:T(8,128)(2,1)} fusion(bf16[96,1000]{1,0:T(8,128)(2,1)S(1)} %bitcast.208, s32[1024]{0:T(1024)S(1)} %pad_clamp_fusion), kind=kCustom, calls=%fused_computation.5.clone | custom fusion | bytes 3075072 | tf_op jit(solution)/shard_map/jit(_take)/gather | solution.py:95
  115.7 2.7 %copy.43 = bf16[768,1000]{0,1:T(8,128)(2,1)} copy(bf16[768,1000]{1,0:T(8,128)(2,1)} %gather_fusion.6) | data formatting | bytes 3072000 | tf_op jit(solution)/shard_map/jit(_take)/gather | solution.py:95
  118.4 1.7 %broadcast_select_fusion = bf16[768,1000]{0,1:T(8,128)(2,1)S(1)} fusion(bf16[768,1000]{0,1:T(8,128)(2,1)} %copy.43, pred[768]{0:T(1024)(128)(4,1)S(1)} %get-tuple-element.18), kind=kLoop, calls=%fused_computation.47 | loop fusion | flops 768000 | bytes 3072768 | tf_op jit(solution)/shard_map/jit(_take)/select_n | solution.py:95
  120.0 0.2 copy-done.2
  120.2 2.0 %convert_multiply_fusion = (f32[768,500]{0,1:T(8,128)}, f32[768,500]{0,1:T(8,128)}) fusion(f32[768,500]{0,1:T(8,128)S(1)} %copy-done.2, bf16[768,1000]{0,1:T(8,128)(2,1)S(1)} %broadcast_select_fusion), kind=kLoop, calls=%fused_computation.43 | loop fusion | flops 1536000 | bytes 6144000 | tf_op jit(solution)/shard_map/mul | solution.py:97
  122.2 3.0 %copy.45 = f32[768,500]{1,0:T(8,128)} copy(f32[768,500]{0,1:T(8,128)} %get-tuple-element.22) | data formatting | bytes 3072000 | tf_op jit(solution)/shard_map/mul | solution.py:97
  125.3 1.9 %bitcast_reduce_fusion = f32[96,500]{1,0:T(8,128)S(1)} fusion(f32[768,500]{1,0:T(8,128)} %copy.45), kind=kLoop, calls=%fused_computation.7 | loop fusion | flops 336000 | bytes 1728000 | tf_op jit(solution)/shard_map/reduce_sum | solution.py:96
  127.2 0.6 fusion.2
  127.7 0.6 fusion.16
  128.3 3.0 %copy.44 = f32[768,500]{1,0:T(8,128)} copy(f32[768,500]{0,1:T(8,128)} %get-tuple-element.23) | data formatting | bytes 3072000 | tf_op jit(solution)/shard_map/mul | solution.py:100
  131.4 1.9 %bitcast_reduce_fusion.1 = f32[96,500]{1,0:T(8,128)S(1)} fusion(f32[768,500]{1,0:T(8,128)} %copy.44), kind=kLoop, calls=%fused_computation.8 | loop fusion | flops 336000 | bytes 1728000 | tf_op jit(solution)/shard_map/reduce_sum | solution.py:99
  133.3 0.6 fusion.18
  133.8 0.6 fusion
  134.7 10.1 %all-reduce = (f32[96,16]{0,1:T(8,128)S(1)}, f32[96,16]{0,1:T(8,128)S(1)}) all-reduce(f32[96,16]{0,1:T(8,128)S(1)} %fusion.81, f32[96,16]{0,1:T(8,128)S(1)} %fusion.82), channel_id=1, replica_groups=mesh['grp'=2,'kb'=4,'gb'=4] {'gb'}, use_global_device_ids=true, to_apply=%region_19.23 | all-reduce | flops 3072 | bytes 24576 | tf_op jit(solution)/shard_map/psum | solution.py:124
  144.9 0.6 fusion.80
  145.5 0.6 fusion.71
  (76 shorter events, 2.8 us)
Async XLA Ops:
  0.0 61.5 %copy-start = (f32[16,500]{1,0:T(8,128)S(1)}, f32[16,500]{1,0:T(8,128)}, u32[]{:S(2)}) copy-start(f32[16,500]{1,0:T(8,128)} %param.23) | copy-start | bytes 96004
  3.0 34.5 %all-to-all-start = ((s32[4,1,24]{2,1,0:T(1,128)}), s32[4,1,24]{2,1,0:T(1,128)S(1)}, u32[]{:S(2)}, u32[]{:S(2)}) async-start(s32[4,1,24]{2,1,0:T(1,128)} %bitcast.10), calls=%async_computation | async-start | bytes 4096 | tf_op jit(solution)/shard_map/all_to_all | solution.py:56
  10.1 5.1 %copy-start.1 = (bf16[2,96,16,500]{3,2,1,0:T(8,128)(2,1)S(1)}, bf16[2,96,16,500]{3,2,1,0:T(8,128)(2,1)}, u32[]{:S(2)}) copy-start(bf16[2,96,16,500]{3,2,1,0:T(8,128)(2,1)} %param.19) | copy-start | bytes 9216004
  16.3 1.5 copy-start.10
  16.3 1.5 %copy-start.9 = (f32[2]{0:T(128)S(1)}, f32[2]{0:T(128)}, u32[]{:S(2)}) copy-start(f32[2]{0:T(128)} %param.18) | copy-start | bytes 28
  19.9 17.3 %copy-start.8 = (s32[96,8]{0,1:T(8,128)S(1)}, s32[96,8]{0,1:T(8,128)}, u32[]{:S(2)}) copy-start(s32[96,8]{0,1:T(8,128)} %param.25) | copy-start | bytes 9220
  24.9 20.3 %copy-start.7 = (f32[500]{0:T(512)S(1)}, f32[500]{0:T(512)}, u32[]{:S(2)}) copy-start(f32[500]{0:T(512)} %param.22) | copy-start | bytes 6004
  41.9 9.6 %all-to-all-start.1 = ((bf16[4,24,1000]{2,1,0:T(8,128)(2,1)}), bf16[4,24,1000]{2,1,0:T(8,128)(2,1)S(1)}, u32[]{:S(2)}, u32[]{:S(2)}) async-start(bf16[4,24,1000]{2,1,0:T(8,128)(2,1)} %bitcast.211), calls=%async_computation.1 | async-start | bytes 393216 | tf_op jit(solution)/shard_map/all_to_all | solution.py:62
  76.6 11.1 %copy-start.4 = (f32[2,96,16]{1,2,0:T(8,128)S(1)}, f32[2,96,16]{1,2,0:T(8,128)}, u32[]{:S(2)}) copy-start(f32[2,96,16]{1,2,0:T(8,128)} %param.17) | copy-start | bytes 36868
  76.6 11.1 %copy-start.5 = (f32[2,96,16]{1,2,0:T(8,128)S(1)}, f32[2,96,16]{1,2,0:T(8,128)}, u32[]{:S(2)}) copy-start(f32[2,96,16]{1,2,0:T(8,128)} %param.21) | copy-start | bytes 36868
  76.6 11.1 %copy-start.6 = (f32[96,16]{0,1:T(8,128)S(1)}, f32[96,16]{0,1:T(8,128)}, u32[]{:S(2)}) copy-start(f32[96,16]{0,1:T(8,128)} %param.20) | copy-start | bytes 18436
  89.9 0.9 copy-start.3
  94.2 15.7 %all-to-all-start.2 = ((bf16[4,24,1000]{2,1,0:T(8,128)(2,1)}), bf16[4,24,1000]{2,1,0:T(8,128)(2,1)S(1)}, u32[]{:S(2)}, u32[]{:S(2)}) async-start(bf16[4,24,1000]{2,1,0:T(8,128)(2,1)} %bitcast.210), calls=%async_computation.2 | async-start | bytes 393216 | tf_op jit(solution)/shard_map/all_to_all | solution.py:62
  118.4 1.9 %copy-start.2 = (f32[768,500]{0,1:T(8,128)S(1)}, f32[768,500]{0,1:T(8,128)}, u32[]{:S(2)}) copy-start(f32[768,500]{0,1:T(8,128)} %get-tuple-element.50) | copy-start | bytes 4608004
where the time goes:
time: 147 us; the launch traced here: 146 us
  blocking collectives  44.8 us (30%)
  local copies, waits for them, and re-layouts  38.6 us (26%)
  other arithmetic  25.9 us (18%)
  matrix products  17.3 us (12%)
  starting transfers between devices  13 us (9%)
  waiting for transfers between devices  6.18 us (4%)
    psum x2, blocking collectives, derivative(): lax.psum((jnp.sum(dens_real, axis=0), jnp.sum(dens_imag, axis=0)), 'kb')  24.5 us
    psum x2, blocking collectives, derivative(): proj_real, proj_imag = lax.psum((proj_real, proj_imag), 'gb')  20.3 us
    gather x4, local copies, waits for them, and re-layouts, derivative(): pulled = jnp.take(received, position, axis=0)  12.5 us
    all_to_all x2, starting transfers between devices, fetch(): lax.all_to_all(outgoing, 'kb', split_axis=0, concat_axis=0, tiled=True)  6.73 us
    all_to_all x1, starting transfers between devices, body(): given = lax.all_to_all(asked, 'kb', split_axis=0, concat_axis=0, tiled=True)  6.32 us
    all_to_all x2, waiting for transfers between devices, fetch(): lax.all_to_all(outgoing, 'kb', split_axis=0, concat_axis=0, tiled=True)  6.18 us
    mul x2, local copies, waits for them, and re-layouts, derivative(): pulled[:, g_local:] * weights  6.07 us
    mul x2, local copies, waits for them, and re-layouts, derivative(): pulled[:, :g_local] * weights  6.05 us
  transfers between devices with their start and end apart: 3, of which 1 were waited for; matrix products, arithmetic and copies ran while one was open for 11% of the time, Pallas kernels for 0%

commit v1 on v0

v1 whole, which is shorter than its diff:
```python
import functools
import math

import jax
import jax.numpy as jnp
from jax import lax
from jax.experimental import pallas as pl
from jax.experimental.pallas import tpu as pltpu
from jax.sharding import PartitionSpec as P

CAP = 24
TIME_STEP = 0.25
LANES = 128
MESH = pl.DeviceIdType.MESH
F32 = jnp.float32
BF16 = jnp.bfloat16


def iota(shape, dim):
    return lax.broadcasted_iota(jnp.int32, shape, dim)


def nn(a, b):
    return lax.dot_general(a, b, (((1,), (0,)), ((), ())), preferred_element_type=F32)


def nt(a, b):
    return lax.dot_general(a, b, (((1,), (1,)), ((), ())), preferred_element_type=F32)


def each(lo, hi, fn):
    if hi - lo <= 8:
        for i in range(lo, hi):
            fn(i)
    else:
        lax.fori_loop(lo, hi, lambda i, c: (fn(i), c)[1], 0)


def picks(rows4):
    wanted = jnp.concatenate(rows4 + rows4, axis=0)
    upper = (iota((LANES, LANES), 0) <= iota((LANES, LANES), 1)).astype(F32).astype(BF16)
    rank = nn(wanted.astype(BF16), upper)
    order = iota((2 * CAP, LANES), 0)
    order = jnp.where(order >= CAP, order - CAP, order).astype(F32) + 1.0
    blocks = []
    for s in range(4):
        hit = (rank[s : s + 1] == order).astype(F32) * wanted[s : s + 1]
        blocks.append(hit)
    return jnp.concatenate(blocks, axis=0)


def kernel(
    n_kb, n_gb, k_rows, pairs, slots, g_local, chunks, scales,
    pulse, state, dens_hbm, coulomb, screened, partners, shells, counts,
    out,
    dens, req_send, req_recv, zb, send, rows, nbuf, ybuf, onehot, weight, scr, coul,
    dens_sem, req_ssem, req_rsem, row_ssem, row_rsem, n_ssem, n_rsem, y_ssem, y_rsem,
):
    exchange_weight, direct_weight, g_scale = scales
    me = lax.axis_index("kb")
    mine = lax.axis_index("gb")
    groups = k_rows * pairs // 256
    per = 256 // pairs
    step = 2
    loads = []
    for i in range(groups // step):
        span = pl.ds(i * step * per, step * per)
        cp = pltpu.make_async_copy(dens_hbm.at[:, span], dens.at[:, span], dens_sem.at[i])
        cp.start()
        loads.append(cp)

    barrier = pltpu.get_barrier_semaphore()

    def greet_kb(i):
        pl.semaphore_signal(barrier, inc=1, device_id={"kb": lax.rem(me + i, n_kb)}, device_id_type=MESH)

    def greet_gb(i):
        pl.semaphore_signal(barrier, inc=1, device_id={"gb": lax.rem(mine + i, n_gb)}, device_id_type=MESH)

    each(1, n_kb, greet_kb)
    each(1, n_gb, greet_gb)

    span = n_kb * k_rows
    rel = partners[...] - me * k_rows
    rel = jnp.where(rel < 0, rel + span, rel)
    half_at = (n_kb // 2) * k_rows
    last_at = (n_kb - 1) * k_rows
    key = jnp.where(
        rel < k_rows,
        rel,
        jnp.where(
            rel >= last_at,
            rel - last_at + LANES,
            jnp.where(rel < 2 * k_rows, rel - k_rows + 2 * LANES, rel - half_at + 3 * LANES),
        ),
    )
    first = key[:, 0:1]
    mine4 = []
    for s in range(4):
        hit = (first == iota((k_rows, LANES), 1) + s * LANES).astype(F32)
        mine4.append(jnp.max(hit, axis=0, keepdims=True))
    for s in range(1, 4):
        req_send[s - 1] = jnp.broadcast_to(mine4[s], (8, LANES))

    pl.semaphore_wait(barrier, n_kb - 1 + n_gb - 1)

    sources = [None, lax.rem(me + n_kb - 1, n_kb), lax.rem(me + 1, n_kb), lax.rem(me + n_kb // 2, n_kb)]
    targets = [None, lax.rem(me + 1, n_kb), lax.rem(me + n_kb - 1, n_kb), lax.rem(me + n_kb // 2, n_kb)]
    reqs = []
    for s in range(1, 4):
        cp = pltpu.make_async_remote_copy(
            req_send.at[s - 1], req_recv.at[s - 1], req_ssem.at[s - 1], req_rsem.at[s - 1],
            device_id={"kb": sources[s]}, device_id_type=MESH,
        )
        cp.start()
        reqs.append(cp)

    own = picks(mine4)
    cols = 8 * CAP
    number = iota((8, LANES), 1).astype(F32).astype(BF16)
    at = iota((1, cols), 1)
    slot_at = (at >= 2 * CAP).astype(jnp.int32) + (at >= 4 * CAP).astype(jnp.int32) + (at >= 6 * CAP).astype(jnp.int32)
    imag_at = (at - slot_at * 2 * CAP >= CAP).astype(jnp.int32)
    wanted_key = nt(number, own.astype(BF16))[0:1].astype(jnp.int32) + slot_at * LANES
    scr[...] = jnp.zeros_like(scr)
    scr[:, 0:g_local] = screened[...]
    coul[...] = jnp.zeros_like(coul)
    coul[:, 0:g_local] = coulomb[...] * exchange_weight
    zb[...] = jnp.zeros_like(zb)
    hi = scr[...].astype(BF16)
    rest = scr[...] - hi.astype(F32)
    mid = rest.astype(BF16)
    low = (rest - mid.astype(F32)).astype(BF16)
    kinds = screened.shape[0]
    for j in range(slots):
        hit = key[:, j : j + 1] == wanted_key
        onehot[j * 2 * k_rows : j * 2 * k_rows + k_rows] = (
            jnp.where(imag_at == 0, hit.astype(F32), 0.0).astype(BF16)
        )
        onehot[j * 2 * k_rows + k_rows : (j + 1) * 2 * k_rows] = (
            jnp.where(imag_at == 1, hit.astype(F32), 0.0).astype(BF16)
        )
        kind = (shells[:, j : j + 1] == iota((k_rows, kinds), 1)).astype(F32)
        kind = jnp.where(counts[...] > j, kind, 0.0).astype(BF16)
        weight[j] = nn(kind, hi) + (nn(kind, mid) + nn(kind, low))

    for cp in reqs:
        cp.wait()
    given = picks([mine4[0]] + [req_recv[s][0:1] for s in range(3)])
    row_at = iota((cols, 1), 0)
    row_slot = (row_at >= 2 * CAP).astype(jnp.int32) + (row_at >= 4 * CAP).astype(jnp.int32) + (row_at >= 6 * CAP).astype(jnp.int32)
    row_imag = row_at - row_slot * 2 * CAP >= CAP
    choose = jnp.concatenate(
        [jnp.where(row_imag, 0.0, given), jnp.where(row_imag, given, 0.0)], axis=1
    ).astype(BF16)

    diag = iota((per, 256), 1) // pairs == iota((per, 256), 0)
    starts = [sum(chunks[:i]) for i in range(len(chunks))]

    def section(t, ar, ai):
        left, right = [], []
        for g in range(groups):
            br = jnp.where(diag, jnp.broadcast_to(ar[g : g + 1], (per, 256)), 0.0).astype(BF16)
            bi = jnp.where(diag, jnp.broadcast_to(ai[g : g + 1], (per, 256)), 0.0).astype(BF16)
            left.append(jnp.concatenate([br, bi], axis=0))
            right.append(jnp.concatenate([-bi, br], axis=0))
        row_copies = []
        n_copies = []
        for c, width in enumerate(chunks):
            lo = starts[c]
            real = min(width, g_local - lo)
            sr = jnp.zeros((1, real), F32)
            si = jnp.zeros((1, real), F32)
            for g in range(groups):
                if t == 0 and c == 0 and g % step == 0:
                    loads[g // step].wait()
                mr = dens[0, g * per : (g + 1) * per, :, lo : lo + real].reshape(256, real)
                mi = dens[1, g * per : (g + 1) * per, :, lo : lo + real].reshape(256, real)
                z = nn(left[g], mr) + nn(right[g], mi)
                sr = sr + jnp.sum(z[0:per], axis=0, keepdims=True)
                si = si + jnp.sum(z[per : 2 * per], axis=0, keepdims=True)
                zb[t, g * per : (g + 1) * per, lo : lo + real] = z[0:per].astype(BF16)
                zb[t, LANES + g * per : LANES + (g + 1) * per, lo : lo + real] = z[per : 2 * per].astype(BF16)
            if real < width:
                nbuf[t, c, pl.ds(me, 1)] = jnp.zeros((1, 2, width), F32)
            nbuf[t, c, pl.ds(me, 1), :, 0:real] = jnp.concatenate([sr, si], axis=0)[None]

            def n_copy(i, c=c):
                return pltpu.make_async_remote_copy(
                    nbuf.at[t, c, me], nbuf.at[t, c, me], n_ssem.at[t, c, i], n_rsem.at[t, c, i],
                    device_id={"kb": lax.rem(me + i, n_kb)}, device_id_type=MESH,
                )

            each(1, n_kb, lambda i: n_copy(i).start())
            n_copies.append(n_copy)
            picked = nn(choose, zb[t, :, lo : lo + width]).astype(BF16)
            started = []
            for s in range(1, 4):
                send[t, c, s - 1] = picked[s * 2 * CAP : (s + 1) * 2 * CAP]
            for s in (3, 1, 2):
                cp = pltpu.make_async_remote_copy(
                    send.at[t, c, s - 1], rows.at[t, c, s], row_ssem.at[t, c, s - 1], row_rsem.at[t, c, s - 1],
                    device_id={"kb": targets[s]}, device_id_type=MESH,
                )
                cp.start()
                started.append(cp)
            rows[t, c, 0] = picked[0 : 2 * CAP]
            row_copies.append(started)

        forces = []
        for c, width in enumerate(chunks):
            lo = starts[c]
            for cp in row_copies[c]:
                cp.wait()
            pulled = nn(onehot[...], rows[t, c].reshape(cols, width))
            sum_r = jnp.zeros((k_rows, width), F32)
            sum_i = jnp.zeros((k_rows, width), F32)
            for j in range(slots):
                w = weight[j, :, lo : lo + width]
                sum_r = sum_r + pulled[j * 2 * k_rows : j * 2 * k_rows + k_rows] * w
                sum_i = sum_i + pulled[j * 2 * k_rows + k_rows : (j + 1) * 2 * k_rows] * w
            each(1, n_kb, lambda i: n_copies[c](i).wait())
            total = lax.fori_loop(0, n_kb, lambda i, a: a + nbuf[t, c, i], jnp.zeros((2, width), F32))
            total = total * coul[:, lo : lo + width]
            forces.append(
                (
                    (total[0:1] - direct_weight * sum_r).astype(BF16),
                    (total[1:2] - direct_weight * sum_i).astype(BF16),
                )
            )

        for g in range(groups):
            y = jnp.zeros((2 * per, 256), F32)
            for c, width in enumerate(chunks):
                lo = starts[c]
                real = min(width, g_local - lo)
                fr = forces[c][0][g * per : (g + 1) * per, 0:real]
                fi = forces[c][1][g * per : (g + 1) * per, 0:real]
                mr = dens[0, g * per : (g + 1) * per, :, lo : lo + real].reshape(256, real)
                mi = dens[1, g * per : (g + 1) * per, :, lo : lo + real].reshape(256, real)
                y = y + nt(jnp.concatenate([fr, fi], axis=0), mr) + nt(jnp.concatenate([fi, -fr], axis=0), mi)
            yr = jnp.sum(jnp.where(diag, y[0:per], 0.0), axis=0, keepdims=True)
            yi = jnp.sum(jnp.where(diag, y[per : 2 * per], 0.0), axis=0, keepdims=True)
            ybuf[t, pl.ds(mine, 1), 0, g : g + 1] = yr[None]
            ybuf[t, pl.ds(mine, 1), 1, g : g + 1] = yi[None]

        def y_copy(i):
            return pltpu.make_async_remote_copy(
                ybuf.at[t, mine], ybuf.at[t, mine], y_ssem.at[t, i], y_rsem.at[t, i],
                device_id={"gb": lax.rem(mine + i, n_gb)}, device_id_type=MESH,
            )

        each(1, n_gb, lambda i: y_copy(i).start())
        each(1, n_gb, lambda i: y_copy(i).wait())
        yr = ybuf[t, 0, 0]
        yi = ybuf[t, 0, 1]
        for i in range(1, n_gb):
            yr = yr + ybuf[t, i, 0]
            yi = yi + ybuf[t, i, 1]
        field = pulse[t]
        dr = state[4] * ai + yi * g_scale - field * state[3]
        di = -(state[4] * ar + yr * g_scale - field * state[2])
        return dr, di

    ar = state[0]
    ai = state[1]
    dr, di = section(0, ar, ai)
    dr, di = section(1, ar + 0.5 * TIME_STEP * dr, ai + 0.5 * TIME_STEP * di)
    out[0] = ar + TIME_STEP * dr
    out[1] = ai + TIME_STEP * di


def body(amplitudes, pulse_field, pair_density, energies, dipoles, coulomb, screened, partners, shells, counts):
    k_rows, slots = partners.shape
    pairs = amplitudes.shape[2]
    g_local = coulomb.shape[0]
    n_kb = lax.axis_size("kb")
    n_gb = lax.axis_size("gb")
    groups = k_rows * pairs // 256
    width = -(-g_local // 256) * 256
    chunks = [256] * (width // 256)
    scales = (
        2.0 / math.sqrt(pairs * k_rows * n_kb),
        1.0 / math.sqrt(pairs * slots),
        1.0 / math.sqrt(g_local * n_gb),
    )
    state = jnp.concatenate([amplitudes, dipoles, energies[None]], axis=0).reshape(5, groups, 256)
    nch = len(chunks)
    vmem = pl.BlockSpec(memory_space=pltpu.VMEM)
    dma = pltpu.SemaphoreType.DMA
    result = pl.pallas_call(
        functools.partial(kernel, n_kb, n_gb, k_rows, pairs, slots, g_local, chunks, scales),
        out_shape=jax.ShapeDtypeStruct((2, groups, 256), F32),
        in_specs=[pl.BlockSpec(memory_space=pltpu.SMEM), vmem, pl.BlockSpec(memory_space=pl.ANY)] + [vmem] * 5,
        out_specs=vmem,
        scratch_shapes=[
            pltpu.VMEM(pair_density.shape, BF16),
            pltpu.VMEM((3, 8, LANES), F32),
            pltpu.VMEM((3, 8, LANES), F32),
            pltpu.VMEM((2, 2 * LANES, width), BF16),
            pltpu.VMEM((2, nch, 3, 2 * CAP, 256), BF16),
            pltpu.VMEM((2, nch, 4, 2 * CAP, 256), BF16),
            pltpu.VMEM((2, nch, n_kb, 2, 256), F32),
            pltpu.VMEM((2, n_gb, 2, groups, 256), F32),
            pltpu.VMEM((slots * 2 * k_rows, 8 * CAP), BF16),
            pltpu.VMEM((slots, k_rows, width), F32),
            pltpu.VMEM((screened.shape[0], width), F32),
            pltpu.VMEM((1, width), F32),
            dma((groups,)),
            dma((3,)),
            dma((3,)),
            dma((2, nch, 3)),
            dma((2, nch, 3)),
            dma((2, nch, n_kb)),
            dma((2, nch, n_kb)),
            dma((2, n_gb)),
            dma((2, n_gb)),
        ],
        compiler_params=pltpu.CompilerParams(
            collective_id=0, has_side_effects=True, vmem_limit_bytes=48 * 1024 * 1024
        ),
    )(
        pulse_field, state, pair_density, coulomb[None, :], screened, partners, shells, counts[:, None]
    )
    return result.reshape(2, k_rows, pairs)


def solution(mesh):
    in_specs = (
        P("grp", "kb", None),
        P("grp"),
        P(None, "kb", None, "gb"),
        P("kb", None),
        P(None, "kb", None),
        P("gb"),
        P(None, "gb"),
        P("kb", None),
        P("kb", None),
        P("kb"),
    )
    out_specs = P("grp", "kb", None)
    return jax.shard_map(body, mesh=mesh, in_specs=in_specs, out_specs=out_specs, check_vma=False)
```

time: 147 us -> 42.2 us (0.29)
  blocking collectives: 44.8 us -> 0 us
  Pallas kernels: 0 us -> 31.9 us
  local copies, waits for them, and re-layouts: 38.6 us -> 9.74 us
  other arithmetic: 25.9 us -> 0.01 us
  matrix products: 17.3 us -> 0 us
  starting transfers between devices: 13 us -> 0 us
  waiting for transfers between devices: 6.18 us -> 0 us
    psum x4 -> x0, blocking collectives: 44.8 us -> none  [the longest x2 24.5 us: derivative(): lax.psum((jnp.sum(dens_real, axis=0), jnp.sum(dens_imag, axis=0)), 'kb')]
    pallas_call x0 -> x1, Pallas kernels: none -> 31.9 us  [body(): pl.pallas_call(functools.partial(kernel, n_kb, n_gb, k_rows, pairs, slots...]
    gather x9 -> x0, local copies, waits for them, and re-layouts: 22.9 us -> none  [the longest x4 12.5 us: derivative(): pulled = jnp.take(received, position, axis=0)]
    dot_general x17 -> x0, matrix products: 17.3 us -> none  [the longest x1 3.46 us: body(): jnp.dot(shell_onehot, screened, precision=lax.Precision.HIGHEST)]
    all_to_all x3 -> x0, starting transfers between devices: 13 us -> none  [the longest x2 6.73 us: fetch(): lax.all_to_all(outgoing, 'kb', split_axis=0, concat_axis=0, tiled=True)]
    mul x6 -> x0, local copies, waits for them, and re-layouts: 12.3 us -> none  [the longest x2 6.07 us: derivative(): pulled[:, g_local:] * weights]
    reduce_sum x10 -> x0, other arithmetic: 9.83 us -> none  [the longest x2 3.72 us: derivative(): jnp.sum((pulled[:, :g_local] * weights).reshape(k_rows, partner_slots, g_...]
    select_n x9 -> x0, other arithmetic: 8.63 us -> none  [the longest x3 3.37 us: fetch(): jnp.take(sent_rows, given.reshape(-1), axis=0)]
  transfers between devices with their start and end apart: 3 -> 0, of which waited for: 1 -> 0; matrix products, arithmetic and copies ran while one was open for 11% -> 0% of each run, Pallas kernels for 0% -> 0%
where the time goes in v1:
time: 42.2 us; the launch traced here: 41.7 us
  Pallas kernels  31.9 us (76%)
  local copies, waits for them, and re-layouts  9.74 us (23%)
    pallas_call x1, Pallas kernels, body(): pl.pallas_call(functools.partial(kernel, n_kb, n_gb, k_rows, pairs, slots...  31.9 us
    unnamed x13, local copies, waits for them, and re-layouts  7.94 us

profile of v1, /device:TPU:0, one launch (start us, length us, event | category | flops | bytes accessed | tf_op | source)
XLA Modules:
  0.0 41.7 jit_solution(13582089830719554185)
XLA Ops:
  0.0 0.8 %copy.18 = f32[2,96,16]{2,1,0:T(8,128)S(1)} copy(f32[2,96,16]{1,2,0:T(8,128)} %param.10) | data formatting | bytes 24576 | tf_op args[0]
  0.8 0.1 concatenate.10
  0.9 0.8 %copy.19 = f32[2,96,16]{2,1,0:T(8,128)S(1)} copy(f32[2,96,16]{1,2,0:T(8,128)} %param.14) | data formatting | bytes 24576 | tf_op args[4]
  1.7 0.1 concatenate.11
  1.8 0.8 %copy.20 = f32[96,16]{1,0:T(8,128)S(1)} copy(f32[96,16]{0,1:T(8,128)} %param.13) | data formatting | bytes 12288 | tf_op args[3]
  2.6 0.1 concatenate.12
  2.7 0.8 %copy.21.partners = s32[96,8]{1,0:T(8,128)S(1)} copy(s32[96,8]{0,1:T(8,128)} %param.17) | data formatting | bytes 6144 | tf_op args[7]
  3.5 0.8 %copy.22.shells = s32[96,8]{1,0:T(8,128)S(1)} copy(s32[96,8]{0,1:T(8,128)} %param.18) | data formatting | bytes 6144 | tf_op args[8]
  4.3 0.8 %copy.23.counts = s32[96,1]{1,0:T(8,128)S(1)} copy(s32[96,1]{0,1:T(1,128)} %bitcast.3) | data formatting | bytes 768 | tf_op jit(solution)/shard_map/broadcast_in_dim | solution.py:323
  5.0 0.0 copy-start
  5.0 1.9 %copy-done = bf16[2,96,16,500]{3,2,1,0:T(8,128)(2,1)S(1)} copy-done((bf16[2,96,16,500]{3,2,1,0:T(8,128)(2,1)S(1)}, bf16[2,96,16,500]{3,2,1,0:T(8,128)(2,1)}, u32[]{:S(2)}) %copy-start) | copy-done | bytes 3072024
  6.9 0.0 copy-start.1
  6.9 0.8 %copy-done.1 = f32[16,500]{1,0:T(8,128)S(1)} copy-done((f32[16,500]{1,0:T(8,128)S(1)}, f32[16,500]{1,0:T(8,128)}, u32[]{:S(2)}) %copy-start.1) | copy-done | bytes 32024
  7.7 0.0 copy-start.2
  7.7 0.7 %copy-done.2 = f32[500]{0:T(512)S(1)} copy-done((f32[500]{0:T(512)S(1)}, f32[500]{0:T(512)}, u32[]{:S(2)}) %copy-start.2) | copy-done | bytes 2024
  8.4 0.0 copy-start.3
  8.4 0.7 %copy-done.3 = f32[2]{0:T(128)S(1)} copy-done((f32[2]{0:T(128)S(1)}, f32[2]{0:T(128)}, u32[]{:S(2)}) %copy-start.3) | copy-done | bytes 32
  9.0 31.9 %shard_map.100 = f32[2,6,256]{2,1,0:T(8,128)S(1)} custom-call(f32[2]{0:T(128)S(1)} %copy-done.3, f32[5,6,256]{2,1,0:T(8,128)S(1)} %pad_maximum_fusion.state, bf16[2,96,16,500]{3,2,1,0:T(8,128)(2,1)S(1)} %copy-done, f32[1,500]{1,0:T(1,128)S(1)} %bitcast.2, f32[16,500]{1,0:T(8,128)S(1)} %copy-done.1, s32[96,8]{1,0:T(8,128)S(1)} %copy.21.partners, ...), custom_call_target="tpu_custom_call" | custom-call | tf_op jit(solution)/shard_map/pallas_call | solution.py:291
  41.0 0.1 reshape.8
  41.1 0.7 %copy.24 = f32[2,96,16]{1,2,0:T(8,128)} copy(f32[2,96,16]{2,1,0:T(8,128)S(1)} %reshape.8) | data formatting | bytes 24576 | tf_op jit(solution)/shard_map/reshape | solution.py:325
  (1 shorter events, 0.0 us)
Async XLA Ops:
  5.0 1.9 %copy-start = (bf16[2,96,16,500]{3,2,1,0:T(8,128)(2,1)S(1)}, bf16[2,96,16,500]{3,2,1,0:T(8,128)(2,1)}, u32[]{:S(2)}) copy-start(bf16[2,96,16,500]{3,2,1,0:T(8,128)(2,1)} %dens_hbm.1) | copy-start | bytes 9216004
  6.9 0.8 %copy-start.1 = (f32[16,500]{1,0:T(8,128)S(1)}, f32[16,500]{1,0:T(8,128)}, u32[]{:S(2)}) copy-start(f32[16,500]{1,0:T(8,128)} %screened.1) | copy-start | bytes 96004
  7.7 0.7 %copy-start.2 = (f32[500]{0:T(512)S(1)}, f32[500]{0:T(512)}, u32[]{:S(2)}) copy-start(f32[500]{0:T(512)} %param.15) | copy-start | bytes 6004
  8.4 0.7 %copy-start.3 = (f32[2]{0:T(128)S(1)}, f32[2]{0:T(128)}, u32[]{:S(2)}) copy-start(f32[2]{0:T(128)} %pulse.1) | copy-start | bytes 28

commit v2 on v1

--- a/solution.py
+++ b/solution.py
@@ -51,8 +51,9 @@
 
 def kernel(
     n_kb, n_gb, k_rows, pairs, slots, g_local, chunks, scales,
-    pulse, state, dens_hbm, coulomb, screened, partners, shells, counts,
+    pulse, amps_hbm, dens_hbm, energies_hbm, dipoles_hbm, coulomb_hbm, screened_hbm, partners_hbm, shells_hbm, counts_hbm,
     out,
+    amps, energies, dipoles, coulomb, screened, partners, shells, counts, small_sem,
     dens, req_send, req_recv, zb, send, rows, nbuf, ybuf, onehot, weight, scr, coul,
     dens_sem, req_ssem, req_rsem, row_ssem, row_rsem, n_ssem, n_rsem, y_ssem, y_rsem,
 ):
@@ -62,6 +63,21 @@
     groups = k_rows * pairs // 256
     per = 256 // pairs
     step = 2
+    small = {}
+    for i, (name, src, dst) in enumerate(
+        (
+            ("partners", partners_hbm, partners),
+            ("amps", amps_hbm, amps),
+            ("screened", screened_hbm, screened),
+            ("shells", shells_hbm, shells),
+            ("counts", counts_hbm, counts),
+            ("coulomb", coulomb_hbm, coulomb),
+            ("energies", energies_hbm, energies),
+            ("dipoles", dipoles_hbm, dipoles),
+        )
+    ):
+        small[name] = pltpu.make_async_copy(src, dst, small_sem.at[i])
+        small[name].start()
     loads = []
     for i in range(groups // step):
         span = pl.ds(i * step * per, step * per)
@@ -81,7 +97,8 @@
     each(1, n_gb, greet_gb)
 
     span = n_kb * k_rows
-    rel = partners[...] - me * k_rows
+    small["partners"].wait()
+    rel = partners[...].T - me * k_rows
     rel = jnp.where(rel < 0, rel + span, rel)
     half_at = (n_kb // 2) * k_rows
     last_at = (n_kb - 1) * k_rows
@@ -123,6 +140,10 @@
     imag_at = (at - slot_at * 2 * CAP >= CAP).astype(jnp.int32)
     wanted_key = nt(number, own.astype(BF16))[0:1].astype(jnp.int32) + slot_at * LANES
     scr[...] = jnp.zeros_like(scr)
+    for name in ("screened", "coulomb", "shells", "counts"):
+        small[name].wait()
+    kind_of = shells[...].T
+    live = jnp.broadcast_to(counts[...], (8, k_rows)).T[:, 0:1]
     scr[:, 0:g_local] = screened[...]
     coul[...] = jnp.zeros_like(coul)
     coul[:, 0:g_local] = coulomb[...] * exchange_weight
@@ -140,8 +161,8 @@
         onehot[j * 2 * k_rows + k_rows : (j + 1) * 2 * k_rows] = (
             jnp.where(imag_at == 1, hit.astype(F32), 0.0).astype(BF16)
         )
-        kind = (shells[:, j : j + 1] == iota((k_rows, kinds), 1)).astype(F32)
-        kind = jnp.where(counts[...] > j, kind, 0.0).astype(BF16)
+        kind = (kind_of[:, j : j + 1] == iota((k_rows, kinds), 1)).astype(F32)
+        kind = jnp.where(live > j, kind, 0.0).astype(BF16)
         weight[j] = nn(kind, hi) + (nn(kind, mid) + nn(kind, low))
 
     for cp in reqs:
@@ -156,6 +177,31 @@
 
     diag = iota((per, 256), 1) // pairs == iota((per, 256), 0)
     starts = [sum(chunks[:i]) for i in range(len(chunks))]
+
+    lane_pair = iota((pairs, 256), 1)
+    spread = (lane_pair - lane_pair // pairs * pairs == iota((pairs, 256), 0)).astype(F32)
+    spread = jnp.concatenate([spread] * 3, axis=0).astype(BF16)
+
+    def flat(x):
+        a = x.astype(BF16)
+        b = x - a.astype(F32)
+        c = b.astype(BF16)
+        d = (b - c.astype(F32)).astype(BF16)
+        parts = jnp.concatenate([a, c, d], axis=0)
+        wide = lax.dot_general(parts, spread, (((0,), (0,)), ((), ())), preferred_element_type=F32)
+        return jnp.concatenate(
+            [
+                jnp.sum(jnp.where(diag, wide[g * per : (g + 1) * per], 0.0), axis=0, keepdims=True)
+                for g in range(groups)
+            ],
+            axis=0,
+        )
+
+    for name in ("amps", "energies", "dipoles"):
+        small[name].wait()
+    energy = flat(energies[...])
+    dipole_r = flat(dipoles[0])
+    dipole_i = flat(dipoles[1])
 
     def section(t, ar, ai):
         left, right = [], []
@@ -258,12 +304,12 @@
             yr = yr + ybuf[t, i, 0]
             yi = yi + ybuf[t, i, 1]
         field = pulse[t]
-        dr = state[4] * ai + yi * g_scale - field * state[3]
-        di = -(state[4] * ar + yr * g_scale - field * state[2])
+        dr = energy * ai + yi * g_scale - field * dipole_i
+        di = -(energy * ar + yr * g_scale - field * dipole_r)
         return dr, di
 
-    ar = state[0]
-    ai = state[1]
+    ar = flat(amps[0])
+    ai = flat(amps[1])
     dr, di = section(0, ar, ai)
     dr, di = section(1, ar + 0.5 * TIME_STEP * dr, ai + 0.5 * TIME_STEP * di)
     out[0] = ar + TIME_STEP * dr
@@ -284,16 +330,24 @@
         1.0 / math.sqrt(pairs * slots),
         1.0 / math.sqrt(g_local * n_gb),
     )
-    state = jnp.concatenate([amplitudes, dipoles, energies[None]], axis=0).reshape(5, groups, 256)
     nch = len(chunks)
     vmem = pl.BlockSpec(memory_space=pltpu.VMEM)
     dma = pltpu.SemaphoreType.DMA
     result = pl.pallas_call(
         functools.partial(kernel, n_kb, n_gb, k_rows, pairs, slots, g_local, chunks, scales),
         out_shape=jax.ShapeDtypeStruct((2, groups, 256), F32),
-        in_specs=[pl.BlockSpec(memory_space=pltpu.SMEM), vmem, pl.BlockSpec(memory_space=pl.ANY)] + [vmem] * 5,
+        in_specs=[pl.BlockSpec(memory_space=pltpu.SMEM)] + [pl.BlockSpec(memory_space=pltpu.HBM)] * 9,
         out_specs=vmem,
         scratch_shapes=[
+            pltpu.VMEM((2, pairs, k_rows), F32),
+            pltpu.VMEM((pairs, k_rows), F32),
+            pltpu.VMEM((2, pairs, k_rows), F32),
+            pltpu.VMEM((1, g_local), F32),
+            pltpu.VMEM(screened.shape, F32),
+            pltpu.VMEM((slots, k_rows), jnp.int32),
+            pltpu.VMEM((slots, k_rows), jnp.int32),
+            pltpu.VMEM((1, k_rows), jnp.int32),
+            dma((8,)),
             pltpu.VMEM(pair_density.shape, BF16),
             pltpu.VMEM((3, 8, LANES), F32),
             pltpu.VMEM((3, 8, LANES), F32),
@@ -317,10 +371,19 @@
             dma((2, n_gb)),
         ],
         compiler_params=pltpu.CompilerParams(
-            collective_id=0, has_side_effects=True, vmem_limit_bytes=48 * 1024 * 1024
+            collective_id=0, has_side_effects=True, vmem_limit_bytes=63 * 1024 * 1024
         ),
     )(
-        pulse_field, state, pair_density, coulomb[None, :], screened, partners, shells, counts[:, None]
+        pulse_field,
+        jnp.transpose(amplitudes, (0, 2, 1)),
+        pair_density,
+        energies.T,
+        jnp.transpose(dipoles, (0, 2, 1)),
+        coulomb[None, :],
+        screened,
+        partners.T,
+        shells.T,
+        counts[None, :],
     )
     return result.reshape(2, k_rows, pairs)
 

time: 42.2 us -> 34.7 us (0.82)
  local copies, waits for them, and re-layouts: 9.74 us -> 1.48 us
  Pallas kernels: 31.9 us -> 32.9 us
    unnamed x13 -> x0, local copies, waits for them, and re-layouts: 7.94 us -> none
    pallas_call x1, Pallas kernels: 31.9 us -> 32.9 us  [body(): pl.pallas_call(functools.partial(kernel, n_kb, n_gb, k_rows, pairs, slots...]
    broadcast_in_dim x1 -> x0, local copies, waits for them, and re-layouts: 0.75 us -> none  [body(): counts[:, None]]
    reshape x2, local copies, waits for them, and re-layouts: 0.76 us -> 1.48 us  [body(): return result.reshape(2, k_rows, pairs)]
where the time goes in v2:
time: 34.7 us; the launch traced here: 34.4 us
  Pallas kernels  32.9 us (95%)
  local copies, waits for them, and re-layouts  1.48 us (4%)
    pallas_call x1, Pallas kernels, body(): pl.pallas_call(functools.partial(kernel, n_kb, n_gb, k_rows, pairs, slots...  32.9 us
    reshape x2, local copies, waits for them, and re-layouts, body(): return result.reshape(2, k_rows, pairs)  1.48 us

profile of v2, /device:TPU:0, one launch (start us, length us, event | category | flops | bytes accessed | tf_op | source)
XLA Modules:
  0.0 34.4 jit_solution(17611724968168338886)
XLA Ops:
  0.0 32.9 %shard_map.100 = f32[2,6,256]{2,1,0:T(8,128)} custom-call(f32[2]{0:T(128)} %pulse.1, f32[2,16,96]{2,1,0:T(8,128)} %bitcast.7, bf16[2,96,16,500]{3,2,1,0:T(8,128)(2,1)} %dens_hbm.1, f32[16,96]{1,0:T(8,128)} %bitcast.9, f32[2,16,96]{2,1,0:T(8,128)} %bitcast.8, f32[1,500]{1,0:T(1,128)} %bitcast.12, f32[16,500]{1,0:T(8,128)} %screened_hbm.1, s32[8,96]{1,0:T(8,128)} %bitcast.10, ...), custom_call_target="tpu_custom_call" | custom-call | tf_op jit(solution)/shard_map/pallas_call | solution.py:336
  32.9 0.8 %reshape.3 = f32[2,96,16]{2,1,0:T(8,128)S(1)} reshape(f32[2,6,256]{2,1,0:T(8,128)} %shard_map.100) | data formatting | bytes 24576 | tf_op jit(solution)/shard_map/reshape | solution.py:388
  33.7 0.7 %copy.12 = f32[2,96,16]{1,2,0:T(8,128)} copy(f32[2,96,16]{2,1,0:T(8,128)S(1)} %reshape.3) | data formatting | bytes 24576 | tf_op jit(solution)/shard_map/reshape | solution.py:388

commit v3 on v2

v3 whole, which is shorter than its diff:
```python
import functools
import math

import jax
import jax.numpy as jnp
from jax import lax
from jax.experimental import pallas as pl
from jax.experimental.pallas import tpu as pltpu
from jax.sharding import PartitionSpec as P

CAP = 24
TIME_STEP = 0.25
LANES = 128
MESH = pl.DeviceIdType.MESH
F32 = jnp.float32
BF16 = jnp.bfloat16


def iota(shape, dim):
    return lax.broadcasted_iota(jnp.int32, shape, dim)


def nn(a, b):
    return lax.dot_general(a, b, (((1,), (0,)), ((), ())), preferred_element_type=F32)


def nt(a, b):
    return lax.dot_general(a, b, (((1,), (1,)), ((), ())), preferred_element_type=F32)


def each(lo, hi, fn):
    if hi - lo <= 8:
        for i in range(lo, hi):
            fn(i)
    else:
        lax.fori_loop(lo, hi, lambda i, c: (fn(i), c)[1], 0)


def picks(rows4):
    wanted = jnp.concatenate(rows4 + rows4, axis=0)
    upper = (iota((LANES, LANES), 0) <= iota((LANES, LANES), 1)).astype(F32).astype(BF16)
    rank = nn(wanted.astype(BF16), upper)
    order = iota((2 * CAP, LANES), 0)
    order = jnp.where(order >= CAP, order - CAP, order).astype(F32) + 1.0
    blocks = []
    for s in range(4):
        hit = (rank[s : s + 1] == order).astype(F32) * wanted[s : s + 1]
        blocks.append(hit)
    return jnp.concatenate(blocks, axis=0)


def kernel(
    n_kb, n_gb, k_rows, pairs, slots, g_local, chunks, scales,
    pulse, amps_hbm, dens_hbm, energies_hbm, dipoles_hbm, coulomb_hbm, screened_hbm, partners_hbm, shells_hbm, counts_hbm,
    out,
    amps, energies, dipoles, coulomb, screened, partners, shells, counts, small_sem,
    dens, req_send, req_recv, zb, send, rows, nbuf, ybuf, onehot, weight, scr, coul,
    dens_sem, req_ssem, req_rsem, row_ssem, row_rsem, n_ssem, n_rsem, y_ssem, y_rsem,
):
    exchange_weight, direct_weight, g_scale = scales
    me = lax.axis_index("kb")
    mine = lax.axis_index("gb")
    groups = k_rows * pairs // 256
    per = 256 // pairs
    step = 2
    small = {}
    for i, (name, src, dst) in enumerate(
        (
            ("partners", partners_hbm, partners),
            ("amps", amps_hbm, amps),
            ("screened", screened_hbm, screened),
            ("shells", shells_hbm, shells),
            ("counts", counts_hbm, counts),
            ("coulomb", coulomb_hbm, coulomb),
            ("energies", energies_hbm, energies),
            ("dipoles", dipoles_hbm, dipoles),
        )
    ):
        small[name] = pltpu.make_async_copy(src, dst, small_sem.at[i])
        small[name].start()
    loads = []
    for i in range(groups // step):
        span = pl.ds(i * step * per, step * per)
        cp = pltpu.make_async_copy(dens_hbm.at[:, span], dens.at[:, span], dens_sem.at[i])
        cp.start()
        loads.append(cp)

    barrier = pltpu.get_barrier_semaphore()

    def greet_kb(i):
        pl.semaphore_signal(barrier, inc=1, device_id={"kb": lax.rem(me + i, n_kb)}, device_id_type=MESH)

    def greet_gb(i):
        pl.semaphore_signal(barrier, inc=1, device_id={"gb": lax.rem(mine + i, n_gb)}, device_id_type=MESH)

    each(1, n_kb, greet_kb)
    each(1, n_gb, greet_gb)

    span = n_kb * k_rows
    small["partners"].wait()
    rel = partners[...].T - me * k_rows
    rel = jnp.where(rel < 0, rel + span, rel)
    half_at = (n_kb // 2) * k_rows
    last_at = (n_kb - 1) * k_rows
    key = jnp.where(
        rel < k_rows,
        rel,
        jnp.where(
            rel >= last_at,
            rel - last_at + LANES,
            jnp.where(rel < 2 * k_rows, rel - k_rows + 2 * LANES, rel - half_at + 3 * LANES),
        ),
    )
    first = key[:, 0:1]
    mine4 = []
    for s in range(4):
        hit = (first == iota((k_rows, LANES), 1) + s * LANES).astype(F32)
        mine4.append(jnp.max(hit, axis=0, keepdims=True))
    for s in range(1, 4):
        req_send[s - 1] = jnp.broadcast_to(mine4[s], (8, LANES))

    diag = iota((per, 256), 1) // pairs == iota((per, 256), 0)
    starts = [sum(chunks[:i]) for i in range(len(chunks))]
    lane_pair = iota((pairs, 256), 1)
    spread = (lane_pair - lane_pair // pairs * pairs == iota((pairs, 256), 0)).astype(F32)
    spread = jnp.concatenate([spread] * 3, axis=0).astype(BF16)

    def flat(x):
        a = x.astype(BF16)
        b = x - a.astype(F32)
        c = b.astype(BF16)
        d = (b - c.astype(F32)).astype(BF16)
        parts = jnp.concatenate([a, c, d], axis=0)
        wide = lax.dot_general(parts, spread, (((0,), (0,)), ((), ())), preferred_element_type=F32)
        return jnp.concatenate(
            [
                jnp.sum(jnp.where(diag, wide[g * per : (g + 1) * per], 0.0), axis=0, keepdims=True)
                for g in range(groups)
            ],
            axis=0,
        )

    small["amps"].wait()
    ar = flat(amps[0])
    ai = flat(amps[1])
    zb[...] = jnp.zeros_like(zb)
    for t in range(2):
        for h in range(2):
            ybuf[t, h, pl.ds(mine, 1)] = jnp.zeros((1, 8, 256), F32)
        for c in range(len(chunks)):
            nbuf[t, c, pl.ds(me, 1)] = jnp.zeros((1, 2, 256), F32)

    pl.semaphore_wait(barrier, n_kb - 1 + n_gb - 1)

    sources = [None, lax.rem(me + n_kb - 1, n_kb), lax.rem(me + 1, n_kb), lax.rem(me + n_kb // 2, n_kb)]
    targets = [None, lax.rem(me + 1, n_kb), lax.rem(me + n_kb - 1, n_kb), lax.rem(me + n_kb // 2, n_kb)]
    late = []
    reqs = []
    for s in range(1, 4):
        cp = pltpu.make_async_remote_copy(
            req_send.at[s - 1], req_recv.at[s - 1], req_ssem.at[s - 1], req_rsem.at[s - 1],
            device_id={"kb": sources[s]}, device_id_type=MESH,
        )
        cp.start()
        reqs.append(cp)
        late.append(cp.wait_send)

    cols = 8 * CAP
    halves = [range(0, groups // 2), range(groups // 2, groups)]

    def block(part, g, c):
        lo = starts[c]
        real = min(chunks[c], g_local - lo)
        return dens[part, g * per : (g + 1) * per, :, lo : lo + real].reshape(256, real)

    def diagonal(row):
        return jnp.where(diag, jnp.broadcast_to(row, (per, 256)), 0.0).astype(BF16)

    def sides(xr, xi):
        out_sides = []
        for i in range(xr.shape[0]):
            br = diagonal(xr[i : i + 1])
            bi = diagonal(xi[i : i + 1])
            out_sides.append((jnp.concatenate([br, bi], axis=0), jnp.concatenate([-bi, br], axis=0)))
        return out_sides

    def densities(t, c, gs, factors):
        lo = starts[c]
        real = min(chunks[c], g_local - lo)
        total = [jnp.zeros((1, real), F32)] * 2
        for g, (left, right) in zip(gs, factors):
            if t == 0 and c == 0 and g % step == 0:
                loads[g // step].wait()
            z = nn(left, block(0, g, c)) + nn(right, block(1, g, c))
            for part in range(2):
                zp = z[part * per : (part + 1) * per]
                total[part] = total[part] + jnp.sum(zp, axis=0, keepdims=True)
                zb[t, part * LANES + g * per : part * LANES + (g + 1) * per, lo : lo + real] = zp.astype(BF16)
        return jnp.concatenate(total, axis=0)

    def n_copy(t, c, i):
        return pltpu.make_async_remote_copy(
            nbuf.at[t, c, me], nbuf.at[t, c, me], n_ssem.at[t, c, i], n_rsem.at[t, c, i],
            device_id={"kb": lax.rem(me + i, n_kb)}, device_id_type=MESH,
        )

    def send_n(t, c, total):
        nbuf[t, c, pl.ds(me, 1), :, 0 : total.shape[1]] = total[None]
        each(1, n_kb, lambda i: n_copy(t, c, i).start())
        late.append(lambda: each(1, n_kb, lambda i: n_copy(t, c, i).wait_send()))

    def send_rows(t, c, choose):
        lo = starts[c]
        picked = nn(choose, zb[t, :, lo : lo + chunks[c]]).astype(BF16)
        for s in range(1, 4):
            send[t, c, s - 1] = picked[s * 2 * CAP : (s + 1) * 2 * CAP]
        started = []
        for s in (3, 1, 2):
            cp = pltpu.make_async_remote_copy(
                send.at[t, c, s - 1], rows.at[t, c, s], row_ssem.at[t, c, s - 1], row_rsem.at[t, c, s - 1],
                device_id={"kb": targets[s]}, device_id_type=MESH,
            )
            cp.start()
            started.append(cp)
            late.append(cp.wait_send)
        rows[t, c, 0] = picked[0 : 2 * CAP]
        return started

    def y_copy(t, h, i):
        return pltpu.make_async_remote_copy(
            ybuf.at[t, h, mine], ybuf.at[t, h, mine], y_ssem.at[t, h, i], y_rsem.at[t, h, i],
            device_id={"gb": lax.rem(mine + i, n_gb)}, device_id_type=MESH,
        )

    def project(t, row_copies):
        ys = [None] * groups
        for c, width in enumerate(chunks):
            lo = starts[c]
            real = min(width, g_local - lo)
            for cp in row_copies[c]:
                cp.wait_recv()
            pulled = nn(onehot[...], rows[t, c].reshape(cols, width))
            sums = []
            for part in range(2):
                acc = jnp.zeros((k_rows, width), F32)
                for j in range(slots):
                    at = (2 * j + part) * k_rows
                    acc = acc + pulled[at : at + k_rows] * weight[j, :, lo : lo + width]
                sums.append(acc)
            each(1, n_kb, lambda i: n_copy(t, c, i).wait_recv())
            total = lax.fori_loop(0, n_kb, lambda i, a: a + nbuf[t, c, i], jnp.zeros((2, width), F32))
            total = total * coul[:, lo : lo + width]
            fr = (total[0:1] - direct_weight * sums[0]).astype(BF16)[:, 0:real]
            fi = (total[1:2] - direct_weight * sums[1]).astype(BF16)[:, 0:real]
            for h in range(2):
                for i, g in enumerate(halves[h]):
                    cut = slice(g * per, (g + 1) * per)
                    y = nt(jnp.concatenate([fr[cut], fi[cut]], axis=0), block(0, g, c))
                    y = y + nt(jnp.concatenate([fi[cut], -fr[cut]], axis=0), block(1, g, c))
                    ys[g] = y if c == 0 else ys[g] + y
                    if c == len(chunks) - 1:
                        for part in range(2):
                            row = jnp.where(diag, ys[g][part * per : (part + 1) * per], 0.0)
                            at = part * 4 + i
                            ybuf[t, h, pl.ds(mine, 1), at : at + 1] = jnp.sum(row, axis=0, keepdims=True)[None]
                if c == len(chunks) - 1:
                    each(1, n_gb, lambda i: y_copy(t, h, i).start())
                    late.append(lambda h=h: each(1, n_gb, lambda i: y_copy(t, h, i).wait_send()))

    def slope(t, h, xr, xi):
        each(1, n_gb, lambda i: y_copy(t, h, i).wait_recv())
        y = ybuf[t, h, 0]
        for i in range(1, n_gb):
            y = y + ybuf[t, h, i]
        y = y * g_scale
        cut = slice(halves[h][0], halves[h][-1] + 1)
        count = len(halves[h])
        field = pulse[t]
        dr = energy[cut] * xi[cut] + y[4 : 4 + count] - field * dipole_i[cut]
        di = -(energy[cut] * xr[cut] + y[0:count] - field * dipole_r[cut])
        return dr, di

    factors = sides(ar, ai)
    row_copies = []
    choose = None
    for c in range(len(chunks)):
        send_n(0, c, densities(0, c, range(groups), factors))
        if choose is None:
            for cp in reqs:
                cp.wait_recv()
            given = picks([mine4[0]] + [req_recv[s][0:1] for s in range(3)])
            row_at = iota((cols, 1), 0)
            row_slot = sum((row_at >= 2 * CAP * m).astype(jnp.int32) for m in (1, 2, 3))
            row_imag = row_at - row_slot * 2 * CAP >= CAP
            choose = jnp.concatenate(
                [jnp.where(row_imag, 0.0, given), jnp.where(row_imag, given, 0.0)], axis=1
            ).astype(BF16)
        row_copies.append(send_rows(0, c, choose))

    own = picks(mine4)
    number = iota((8, LANES), 1).astype(F32).astype(BF16)
    at = iota((1, cols), 1)
    slot_at = sum((at >= 2 * CAP * m).astype(jnp.int32) for m in (1, 2, 3))
    imag_at = (at - slot_at * 2 * CAP >= CAP).astype(jnp.int32)
    wanted_key = nt(number, own.astype(BF16))[0:1].astype(jnp.int32) + slot_at * LANES
    for name in ("screened", "coulomb", "shells", "counts", "energies", "dipoles"):
        small[name].wait()
    kind_of = shells[...].T
    live = jnp.broadcast_to(counts[...], (8, k_rows)).T[:, 0:1]
    scr[...] = jnp.zeros_like(scr)
    scr[:, 0:g_local] = screened[...]
    coul[...] = jnp.zeros_like(coul)
    coul[:, 0:g_local] = coulomb[...] * exchange_weight
    hi = scr[...].astype(BF16)
    rest = scr[...] - hi.astype(F32)
    mid = rest.astype(BF16)
    low = (rest - mid.astype(F32)).astype(BF16)
    levels = jnp.concatenate([hi, mid, low], axis=0)
    kinds = screened.shape[0]
    for j in range(slots):
        hit = (key[:, j : j + 1] == wanted_key).astype(F32)
        for part in range(2):
            at_row = (2 * j + part) * k_rows
            onehot[at_row : at_row + k_rows] = jnp.where(imag_at == part, hit, 0.0).astype(BF16)
        kind = (kind_of[:, j : j + 1] == iota((k_rows, kinds), 1)).astype(F32)
        kind = jnp.where(live > j, kind, 0.0).astype(BF16)
        weight[j] = nn(jnp.concatenate([kind] * 3, axis=1), levels)
    energy = flat(energies[...])
    dipole_r = flat(dipoles[0])
    dipole_i = flat(dipoles[1])

    project(0, row_copies)

    totals = [None] * len(chunks)
    row_copies = []
    half_r = []
    half_i = []
    for h in range(2):
        cut = slice(halves[h][0], halves[h][-1] + 1)
        dr, di = slope(0, h, ar, ai)
        half_r.append(ar[cut] + 0.5 * TIME_STEP * dr)
        half_i.append(ai[cut] + 0.5 * TIME_STEP * di)
        factors = sides(half_r[h], half_i[h])
        for c in range(len(chunks)):
            part_total = densities(1, c, halves[h], factors)
            if h == 0:
                totals[c] = part_total
            else:
                send_n(1, c, totals[c] + part_total)
                row_copies.append(send_rows(1, c, choose))
    hr = jnp.concatenate(half_r, axis=0)
    hi_amp = jnp.concatenate(half_i, axis=0)
    project(1, row_copies)
    for h in range(2):
        cut = slice(halves[h][0], halves[h][-1] + 1)
        dr, di = slope(1, h, hr, hi_amp)
        out[0, cut] = ar[cut] + TIME_STEP * dr
        out[1, cut] = ai[cut] + TIME_STEP * di
    for wait in late:
        wait()


def body(amplitudes, pulse_field, pair_density, energies, dipoles, coulomb, screened, partners, shells, counts):
    k_rows, slots = partners.shape
    pairs = amplitudes.shape[2]
    g_local = coulomb.shape[0]
    n_kb = lax.axis_size("kb")
    n_gb = lax.axis_size("gb")
    groups = k_rows * pairs // 256
    width = -(-g_local // 256) * 256
    chunks = [256] * (width // 256)
    scales = (
        2.0 / math.sqrt(pairs * k_rows * n_kb),
        1.0 / math.sqrt(pairs * slots),
        1.0 / math.sqrt(g_local * n_gb),
    )
    nch = len(chunks)
    vmem = pl.BlockSpec(memory_space=pltpu.VMEM)
    dma = pltpu.SemaphoreType.DMA
    result = pl.pallas_call(
        functools.partial(kernel, n_kb, n_gb, k_rows, pairs, slots, g_local, chunks, scales),
        out_shape=jax.ShapeDtypeStruct((2, groups, 256), F32),
        in_specs=[pl.BlockSpec(memory_space=pltpu.SMEM)] + [pl.BlockSpec(memory_space=pltpu.HBM)] * 9,
        out_specs=vmem,
        scratch_shapes=[
            pltpu.VMEM((2, pairs, k_rows), F32),
            pltpu.VMEM((pairs, k_rows), F32),
            pltpu.VMEM((2, pairs, k_rows), F32),
            pltpu.VMEM((1, g_local), F32),
            pltpu.VMEM(screened.shape, F32),
            pltpu.VMEM((slots, k_rows), jnp.int32),
            pltpu.VMEM((slots, k_rows), jnp.int32),
            pltpu.VMEM((1, k_rows), jnp.int32),
            dma((8,)),
            pltpu.VMEM(pair_density.shape, BF16),
            pltpu.VMEM((3, 8, LANES), F32),
            pltpu.VMEM((3, 8, LANES), F32),
            pltpu.VMEM((2, 2 * LANES, width), BF16),
            pltpu.VMEM((2, nch, 3, 2 * CAP, 256), BF16),
            pltpu.VMEM((2, nch, 4, 2 * CAP, 256), BF16),
            pltpu.VMEM((2, nch, n_kb, 2, 256), F32),
            pltpu.VMEM((2, 2, n_gb, 8, 256), F32),
            pltpu.VMEM((slots * 2 * k_rows, 8 * CAP), BF16),
            pltpu.VMEM((slots, k_rows, width), F32),
            pltpu.VMEM((screened.shape[0], width), F32),
            pltpu.VMEM((1, width), F32),
            dma((groups,)),
            dma((3,)),
            dma((3,)),
            dma((2, nch, 3)),
            dma((2, nch, 3)),
            dma((2, nch, n_kb)),
            dma((2, nch, n_kb)),
            dma((2, 2, n_gb)),
            dma((2, 2, n_gb)),
        ],
        compiler_params=pltpu.CompilerParams(
            collective_id=0, has_side_effects=True, vmem_limit_bytes=63 * 1024 * 1024
        ),
    )(
        pulse_field,
        jnp.transpose(amplitudes, (0, 2, 1)),
        pair_density,
        energies.T,
        jnp.transpose(dipoles, (0, 2, 1)),
        coulomb[None, :],
        screened,
        partners.T,
        shells.T,
        counts[None, :],
    )
    return result.reshape(2, k_rows, pairs)


def solution(mesh):
    in_specs = (
        P("grp", "kb", None),
        P("grp"),
        P(None, "kb", None, "gb"),
        P("kb", None),
        P(None, "kb", None),
        P("gb"),
        P(None, "gb"),
        P("kb", None),
        P("kb", None),
        P("kb"),
    )
    out_specs = P("grp", "kb", None)
    return jax.shard_map(body, mesh=mesh, in_specs=in_specs, out_specs=out_specs, check_vma=False)
```

time: 34.7 us -> 33.4 us (0.963)
  Pallas kernels: 32.9 us -> 31.7 us
    pallas_call x1, Pallas kernels: 32.9 us -> 31.7 us  [body(): pl.pallas_call(functools.partial(kernel, n_kb, n_gb, k_rows, pairs, slots...]
where the time goes in v3:
time: 33.4 us; the launch traced here: 33.2 us
  Pallas kernels  31.7 us (95%)
  local copies, waits for them, and re-layouts  1.48 us (4%)
    pallas_call x1, Pallas kernels, body(): pl.pallas_call(functools.partial(kernel, n_kb, n_gb, k_rows, pairs, slots...  31.7 us
    reshape x2, local copies, waits for them, and re-layouts, body(): return result.reshape(2, k_rows, pairs)  1.48 us

profile of v3, /device:TPU:0, one launch (start us, length us, event | category | flops | bytes accessed | tf_op | source)
XLA Modules:
  0.0 33.2 jit_solution(898681066357042630)
XLA Ops:
  0.0 31.7 %shard_map.100 = f32[2,6,256]{2,1,0:T(8,128)} custom-call(f32[2]{0:T(128)} %pulse.1, f32[2,16,96]{2,1,0:T(8,128)} %bitcast.7, bf16[2,96,16,500]{3,2,1,0:T(8,128)(2,1)} %dens_hbm.1, f32[16,96]{1,0:T(8,128)} %bitcast.9, f32[2,16,96]{2,1,0:T(8,128)} %bitcast.8, f32[1,500]{1,0:T(1,128)} %bitcast.12, f32[16,500]{1,0:T(8,128)} %screened_hbm.1, s32[8,96]{1,0:T(8,128)} %bitcast.10, ...), custom_call_target="tpu_custom_call" | custom-call | tf_op jit(solution)/shard_map/pallas_call | solution.py:380
  31.7 0.8 %reshape.3 = f32[2,96,16]{2,1,0:T(8,128)S(1)} reshape(f32[2,6,256]{2,1,0:T(8,128)} %shard_map.100) | data formatting | bytes 24576 | tf_op jit(solution)/shard_map/reshape | solution.py:432
  32.5 0.7 %copy.12 = f32[2,96,16]{1,2,0:T(8,128)} copy(f32[2,96,16]{2,1,0:T(8,128)S(1)} %reshape.3) | data formatting | bytes 24576 | tf_op jit(solution)/shard_map/reshape | solution.py:432

commit v4 on v3

--- a/solution.py
+++ b/solution.py
@@ -145,8 +145,7 @@
     ai = flat(amps[1])
     zb[...] = jnp.zeros_like(zb)
     for t in range(2):
-        for h in range(2):
-            ybuf[t, h, pl.ds(mine, 1)] = jnp.zeros((1, 8, 256), F32)
+        ybuf[t, 0, pl.ds(mine, 1)] = jnp.zeros((1, 16, 256), F32)
         for c in range(len(chunks)):
             nbuf[t, c, pl.ds(me, 1)] = jnp.zeros((1, 2, 256), F32)
 
@@ -166,7 +165,7 @@
         late.append(cp.wait_send)
 
     cols = 8 * CAP
-    halves = [range(0, groups // 2), range(groups // 2, groups)]
+    halves = [range(groups)]
 
     def block(part, g, c):
         lo = starts[c]
@@ -248,11 +247,14 @@
                     acc = acc + pulled[at : at + k_rows] * weight[j, :, lo : lo + width]
                 sums.append(acc)
             each(1, n_kb, lambda i: n_copy(t, c, i).wait_recv())
-            total = lax.fori_loop(0, n_kb, lambda i, a: a + nbuf[t, c, i], jnp.zeros((2, width), F32))
+            if n_kb <= 8:
+                total = sum((nbuf[t, c, i] for i in range(1, n_kb)), nbuf[t, c, 0])
+            else:
+                total = lax.fori_loop(0, n_kb, lambda i, a: a + nbuf[t, c, i], jnp.zeros((2, width), F32))
             total = total * coul[:, lo : lo + width]
             fr = (total[0:1] - direct_weight * sums[0]).astype(BF16)[:, 0:real]
             fi = (total[1:2] - direct_weight * sums[1]).astype(BF16)[:, 0:real]
-            for h in range(2):
+            for h in range(len(halves)):
                 for i, g in enumerate(halves[h]):
                     cut = slice(g * per, (g + 1) * per)
                     y = nt(jnp.concatenate([fr[cut], fi[cut]], axis=0), block(0, g, c))
@@ -261,7 +263,7 @@
                     if c == len(chunks) - 1:
                         for part in range(2):
                             row = jnp.where(diag, ys[g][part * per : (part + 1) * per], 0.0)
-                            at = part * 4 + i
+                            at = part * 8 + i
                             ybuf[t, h, pl.ds(mine, 1), at : at + 1] = jnp.sum(row, axis=0, keepdims=True)[None]
                 if c == len(chunks) - 1:
                     each(1, n_gb, lambda i: y_copy(t, h, i).start())
@@ -276,25 +278,24 @@
         cut = slice(halves[h][0], halves[h][-1] + 1)
         count = len(halves[h])
         field = pulse[t]
-        dr = energy[cut] * xi[cut] + y[4 : 4 + count] - field * dipole_i[cut]
+        dr = energy[cut] * xi[cut] + y[8 : 8 + count] - field * dipole_i[cut]
         di = -(energy[cut] * xr[cut] + y[0:count] - field * dipole_r[cut])
         return dr, di
 
     factors = sides(ar, ai)
     row_copies = []
-    choose = None
     for c in range(len(chunks)):
         send_n(0, c, densities(0, c, range(groups), factors))
-        if choose is None:
-            for cp in reqs:
-                cp.wait_recv()
-            given = picks([mine4[0]] + [req_recv[s][0:1] for s in range(3)])
-            row_at = iota((cols, 1), 0)
-            row_slot = sum((row_at >= 2 * CAP * m).astype(jnp.int32) for m in (1, 2, 3))
-            row_imag = row_at - row_slot * 2 * CAP >= CAP
-            choose = jnp.concatenate(
-                [jnp.where(row_imag, 0.0, given), jnp.where(row_imag, given, 0.0)], axis=1
-            ).astype(BF16)
+    for cp in reqs:
+        cp.wait_recv()
+    given = picks([mine4[0]] + [req_recv[s][0:1] for s in range(3)])
+    row_at = iota((cols, 1), 0)
+    row_slot = sum((row_at >= 2 * CAP * m).astype(jnp.int32) for m in (1, 2, 3))
+    row_imag = row_at - row_slot * 2 * CAP >= CAP
+    choose = jnp.concatenate(
+        [jnp.where(row_imag, 0.0, given), jnp.where(row_imag, given, 0.0)], axis=1
+    ).astype(BF16)
+    for c in range(len(chunks)):
         row_copies.append(send_rows(0, c, choose))
 
     own = picks(mine4)
@@ -335,7 +336,7 @@
     row_copies = []
     half_r = []
     half_i = []
-    for h in range(2):
+    for h in range(len(halves)):
         cut = slice(halves[h][0], halves[h][-1] + 1)
         dr, di = slope(0, h, ar, ai)
         half_r.append(ar[cut] + 0.5 * TIME_STEP * dr)
@@ -343,15 +344,15 @@
         factors = sides(half_r[h], half_i[h])
         for c in range(len(chunks)):
             part_total = densities(1, c, halves[h], factors)
-            if h == 0:
+            if h < len(halves) - 1:
                 totals[c] = part_total
             else:
-                send_n(1, c, totals[c] + part_total)
                 row_copies.append(send_rows(1, c, choose))
+                send_n(1, c, part_total if h == 0 else totals[c] + part_total)
     hr = jnp.concatenate(half_r, axis=0)
     hi_amp = jnp.concatenate(half_i, axis=0)
     project(1, row_copies)
-    for h in range(2):
+    for h in range(len(halves)):
         cut = slice(halves[h][0], halves[h][-1] + 1)
         dr, di = slope(1, h, hr, hi_amp)
         out[0, cut] = ar[cut] + TIME_STEP * dr
@@ -399,7 +400,7 @@
             pltpu.VMEM((2, nch, 3, 2 * CAP, 256), BF16),
             pltpu.VMEM((2, nch, 4, 2 * CAP, 256), BF16),
             pltpu.VMEM((2, nch, n_kb, 2, 256), F32),
-            pltpu.VMEM((2, 2, n_gb, 8, 256), F32),
+            pltpu.VMEM((2, 1, n_gb, 16, 256), F32),
             pltpu.VMEM((slots * 2 * k_rows, 8 * CAP), BF16),
             pltpu.VMEM((slots, k_rows, width), F32),
             pltpu.VMEM((screened.shape[0], width), F32),

time: 33.4 us -> 32.8 us (0.982)
  Pallas kernels: 31.7 us -> 31 us
    pallas_call x1, Pallas kernels: 31.7 us -> 31 us  [body(): pl.pallas_call(functools.partial(kernel, n_kb, n_gb, k_rows, pairs, slots...]
where the time goes in v4:
time: 32.8 us; the launch traced here: 32.5 us
  Pallas kernels  31 us (95%)
  local copies, waits for them, and re-layouts  1.48 us (5%)
    pallas_call x1, Pallas kernels, body(): pl.pallas_call(functools.partial(kernel, n_kb, n_gb, k_rows, pairs, slots...  31 us
    reshape x2, local copies, waits for them, and re-layouts, body(): return result.reshape(2, k_rows, pairs)  1.48 us

profile of v4, /device:TPU:0, one launch (start us, length us, event | category | flops | bytes accessed | tf_op | source)
XLA Modules:
  0.0 32.5 jit_solution(630894609258438161)
XLA Ops:
  0.0 31.0 %shard_map.100 = f32[2,6,256]{2,1,0:T(8,128)} custom-call(f32[2]{0:T(128)} %pulse.1, f32[2,16,96]{2,1,0:T(8,128)} %bitcast.7, bf16[2,96,16,500]{3,2,1,0:T(8,128)(2,1)} %dens_hbm.1, f32[16,96]{1,0:T(8,128)} %bitcast.9, f32[2,16,96]{2,1,0:T(8,128)} %bitcast.8, f32[1,500]{1,0:T(1,128)} %bitcast.12, f32[16,500]{1,0:T(8,128)} %screened_hbm.1, s32[8,96]{1,0:T(8,128)} %bitcast.10, ...), custom_call_target="tpu_custom_call" | custom-call | tf_op jit(solution)/shard_map/pallas_call | solution.py:381
  31.0 0.8 %reshape.3 = f32[2,96,16]{2,1,0:T(8,128)S(1)} reshape(f32[2,6,256]{2,1,0:T(8,128)} %shard_map.100) | data formatting | bytes 24576 | tf_op jit(solution)/shard_map/reshape | solution.py:433
  31.8 0.7 %copy.12 = f32[2,96,16]{1,2,0:T(8,128)} copy(f32[2,96,16]{2,1,0:T(8,128)S(1)} %reshape.3) | data formatting | bytes 24576 | tf_op jit(solution)/shard_map/reshape | solution.py:433
